TPU v7x, 32 devices: a whole 2x2x4 slice. The times are simulated.
32 devices in a mesh: slab: 2 (over x), plane: 8 (over z, y), brick: 2 (over core).
Axes of the slice: x: 2, y: 2, z: 4, core: 2. Of those that a mesh axis runs over, the one named last changes fastest.
Arguments:
- camera_rows: bfloat16 [4, 16, 32, 2048], P(None, 'slab', ('plane', 'brick')), parts along dimension 1, may hold values from 0.19921875 to 5
- estimate: float32 [16, 32, 2048], P('slab', None, ('plane', 'brick')), parts along dimension 0, may hold values from 0.2 to 5
- psf_bank: float32 [32, 4, 3, 31], P(('slab', 'plane', 'brick')), parts along dimension 0, may hold values from 0 to 1.25, as said below
- psf_owner: int32 [32], P('slab'), parts along dimension 0, may hold values from 0 to 15, each once
- view_mask: int32 [32, 4], P('slab'), parts along dimension 0, may hold values 0 or 1
Outputs:
- deconvolved: float32 [16, 32, 2048], P('slab', None, ('plane', 'brick')), parts along dimension 0
There are 2 independent parts, one for each index of `slab`. A program takes and returns all parts, laid end to end along the dimension named above; each array names one. Nothing has to cross between parts.
Inputs may be any that keep to these rules, and one draw needn't show every extreme that they name: `psf_owner`: every brick names a different device: the map is a permutation of 0 to 15. `psf_bank`: every tap is positive.
All inputs are finite; a program needn't handle non-finite values.
Results may differ from a plain program's by a relative error of at most 0.0003.
Values may be sent and summed in bfloat16 or wider, within the bound.
A program may use at most 192 MiB of HBM per device.

v0:
```python
import jax
import jax.numpy as jnp
from jax import lax
from jax.sharding import PartitionSpec as P

V = 4
RADIUS = 15
ITERS = 2


BACKGROUND = 0.1
HIGHEST = lax.Precision.HIGHEST


def padded_2(cells, sides, width):
    for axis, dim in sides:
        count = lax.axis_size(axis)
        ends = count - 1
        head = lax.slice_in_dim(cells, 0, width, axis=dim)
        tail = lax.slice_in_dim(cells, cells.shape[dim] - width, cells.shape[dim], axis=dim)
        cells = jnp.concatenate(
            [
                lax.ppermute(tail, axis, [(i, (i + 1) % count) for i in range(ends)]),
                cells,
                lax.ppermute(head, axis, [((i + 1) % count, i) for i in range(ends)]),
            ],
            axis=dim,
        )
    return cells


def banded(profiles, size_in, size_out, offset):
    tap_count = profiles.shape[-1]
    centre = tap_count // 2
    lag_index = (
        jnp.arange(size_in, dtype=jnp.int32)[:, None]
        - jnp.arange(size_out, dtype=jnp.int32)[None, :]
        - offset
        + centre
    )
    one_hot = (
        lag_index[:, :, None] == jnp.arange(tap_count, dtype=jnp.int32)[None, None, :]
    ).astype(jnp.float32)
    return jnp.einsum("ijt,vt->vij", one_hot, profiles, precision=HIGHEST)


def across_columns(volume, band_x):
    if volume.ndim == 3:
        return jnp.einsum("zyi,vij->vzyj", volume, band_x, precision=HIGHEST)
    return jnp.einsum("vzyi,vij->vzyj", volume, band_x, precision=HIGHEST)


def across_rows(volume, band_y):
    view_count, depth_count, row_count, col_count = volume.shape
    block_rows = band_y.shape[2]
    margin = (band_y.shape[1] - block_rows) // 2
    pieces = volume.reshape(view_count, depth_count, row_count // block_rows, block_rows, col_count)
    blanks = jnp.zeros((view_count, depth_count, 1, margin, col_count), jnp.float32)
    before = jnp.concatenate([blanks, pieces[:, :, :-1, block_rows - margin :, :]], axis=2)
    behind = jnp.concatenate([pieces[:, :, 1:, :margin, :], blanks], axis=2)
    windows = jnp.concatenate([before, pieces, behind], axis=3)
    result = jnp.einsum("vzqic,vij->vzqjc", windows, band_y, precision=HIGHEST)
    return result.reshape(view_count, depth_count, row_count, col_count)


def across_depth(volume, band_z):
    return jnp.einsum("vzyc,vzw->vwyc", volume, band_z, precision=HIGHEST)


def separable(volume, bands):
    return across_depth(across_rows(across_columns(volume, bands[0]), bands[1]), bands[2])


def shards(camera_rows, estimate, psf_bank, psf_owner, view_mask):
    regrouped = lax.all_to_all(
        camera_rows, ("plane", "brick"), split_axis=3, concat_axis=2, tiled=True
    )
    position = lax.axis_index(("plane", "brick"))
    brick_ids = jnp.arange(psf_owner.shape[0], dtype=jnp.int32)
    is_mine = brick_ids == position
    owner_id = jnp.sum(jnp.where(is_mine, psf_owner, 0))
    observed = jnp.sum(jnp.where(is_mine[:, None], view_mask, 0), axis=0) > 0
    fitted = lax.all_gather(psf_bank, ("plane", "brick"), axis=0, tiled=True)
    chosen = (brick_ids == owner_id).astype(jnp.float32)
    kernels = jnp.einsum("b,bvat->vat", chosen, fitted, precision=HIGHEST)
    kernels = kernels / jnp.sum(kernels, axis=-1, keepdims=True)
    flipped = kernels[:, :, ::-1]
    depth_size = estimate.shape[0]
    row_size = estimate.shape[1]
    col_size = estimate.shape[2]
    block_size = 128 if row_size % 128 == 0 else row_size

    def make_bands(profiles):
        return (
            banded(profiles[:, 2], col_size + 2 * RADIUS, col_size, RADIUS),
            banded(profiles[:, 1], block_size + 2 * RADIUS, block_size, RADIUS),
            banded(profiles[:, 0], depth_size, depth_size, 0),
        )

    blur_bands = make_bands(kernels)
    back_bands = make_bands(flipped)
    current = estimate
    for iteration in range(ITERS):
        padded = padded_2(current.astype(jnp.bfloat16), ((("plane", "brick"), 2),), RADIUS).astype(
            current.dtype
        )
        blurred = separable(padded, blur_bands)
        quotient = jnp.where(
            observed[:, None, None, None],
            regrouped.astype(jnp.float32) / (blurred + BACKGROUND),
            0.0,
        )
        quotient_wide = padded_2(
            quotient.astype(jnp.bfloat16), ((("plane", "brick"), 3),), RADIUS
        ).astype(quotient.dtype)
        corrected = separable(quotient_wide, back_bands)
        factor = jnp.sum(jnp.where(observed[:, None, None, None], corrected, 1.0), axis=0) / V
        current = current * factor
    return current


def solution(mesh):
    return jax.shard_map(
        shards,
        mesh=mesh,
        in_specs=(
            P(None, "slab", ("plane", "brick"), None),
            P("slab", None, ("plane", "brick")),
            P(("slab", "plane", "brick"), None, None, None),
            P("slab"),
            P("slab", None),
        ),
        out_specs=P("slab", None, ("plane", "brick")),
        check_vma=False,
    )
```

profile of v0, /device:TPU:1, one launch (start us, length us, event | category | flops | bytes accessed | tf_op | source)
XLA Modules:
  0.0 100.3 jit_solution(6253015987272240798)
XLA Ops:
  0.0 6.3 %copy.47 = bf16[4,8,2,2048]{1,0,2,3:T(4,128)(2,1)} copy(bf16[4,8,2,2048]{3,2,1,0:T(2,128)(2,1)} %param.5) | data formatting | bytes 524288 | tf_op args[0]
  6.4 6.5 %reshape.127 = bf16[16,2,4096]{2,1,0:T(2,128)(2,1)} reshape(bf16[2048,2,4,8]{3,2,1,0:T(4,128)(2,1)} %bitcast.116) | data formatting | bytes 524288
  12.8 7.3 %all-to-all-start = ((bf16[16,2,4096]{2,1,0:T(2,128)(2,1)}), bf16[16,2,4096]{2,1,0:T(2,128)(2,1)S(1)}, u32[]{:S(2)}, u32[]{:S(2)}) async-start(bf16[16,2,4096]{2,1,0:T(2,128)(2,1)} %reshape.127), calls=%async_computation | async-start | bytes 524288 | tf_op jit(solution)/shard_map/all_to_all | solution.py:75
  20.3 2.0 %collective-permute-start.1 = (bf16[8,32,15]{2,1,0:T(8,128)(2,1)S(1)}, bf16[8,32,15]{2,1,0:T(8,128)(2,1)S(1)}, u32[]{:S(2)}, u32[]{:S(2)}) collective-permute-start(bf16[8,32,15]{2,1,0:T(8,128)(2,1)S(1)} %get-tuple-element.12), channel_id=1, source_target_pairs={{1,0},{2,1},{3,2},{4,3},{5,4},{6,5},{7,6},{8,7},{9,8},{10,9},{11,1... | collective-permute-start | bytes 23048 | tf_op jit(solution)/shard_map/ppermute | solution.py:25
  22.3 3.5 %collective-permute-start = (bf16[8,32,15]{2,1,0:T(8,128)(2,1)S(1)}, bf16[8,32,15]{2,1,0:T(8,128)(2,1)S(1)}, u32[]{:S(2)}, u32[]{:S(2)}) collective-permute-start(bf16[8,32,15]{2,1,0:T(8,128)(2,1)S(1)} %get-tuple-element.11), channel_id=1, source_target_pairs={{0,1},{1,2},{2,3},{3,4},{4,5},{5,6},{6,7},{7,8},{8,9},{9,10},{10,1... | collective-permute-start | bytes 23048 | tf_op jit(solution)/shard_map/ppermute | solution.py:23
  25.9 20.7 %all_gather.3 = f32[16,4,3,31]{3,1,2,0:T(4,128)S(1)} all-gather(f32[1,4,3,31]{3,1,2,0:T(4,128)S(1)} %copy-done.1), channel_id=1, replica_groups=mesh['slab'=2,'plane'=8,'brick'=2] {'plane','brick'}, dimensions={0}, use_global_device_ids=true | all-gather | bytes 25296 | tf_op jit(solution)/shard_map/all_gather | solution.py:83
  46.6 0.6 select_reduce_fusion.1
  47.2 0.8 fusion.48
  48.2 0.9 fusion.12
  49.1 0.3 convolution_bitcast_fusion.8
  49.4 0.1 select_reduce_fusion
  49.5 0.1 slice.54
  49.6 0.9 fusion.13
  50.5 0.1 slice.48
  50.6 0.3 convolution_bitcast_fusion.9
  50.9 0.4 convolution_bitcast_fusion.10
  51.3 0.1 slice.46
  51.5 0.5 convolution_bitcast_fusion.1
  52.0 0.7 convolution_bitcast_fusion.7
  52.7 5.9 %reshape.128 = bf16[2048,2,4,8]{3,2,1,0:T(4,128)(2,1)} reshape(bf16[16,2,4096]{2,1,0:T(2,128)(2,1)S(1)} %all-to-all-done) | data formatting | bytes 524288
  58.7 5.9 %copy.48 = f32[4,8,2,16,128]{4,1,2,3,0:T(8,128)S(1)} copy(bf16[4,8,2,16,128]{1,0,2,4,3:T(4,128)(2,1)} %bitcast.115) | data formatting | bytes 786432 | tf_op jit(solution)/shard_map/convert_element_type | solution.py:110
  64.6 0.9 fusion.8
  65.5 0.1 fusion.77
  65.6 2.1 %collective-permute-start.3 = (bf16[4,8,32,15]{3,1,2,0:T(8,128)(2,1)S(1)}, bf16[4,8,32,15]{3,1,2,0:T(8,128)(2,1)S(1)}, u32[]{:S(2)}, u32[]{:S(2)}) collective-permute-start(bf16[4,8,32,15]{3,1,2,0:T(8,128)(2,1)S(1)} %get-tuple-element.8), channel_id=1, source_target_pairs={{1,0},{2,1},{3,2},{4,3},{5,4},{6,5},{7,6},{8,7},{9,8},{10,9},{11,1... | collective-permute-start | bytes 92168 | tf_op jit(solution)/shard_map/ppermute | solution.py:25
  67.7 3.5 %collective-permute-start.2 = (bf16[4,8,32,15]{3,1,2,0:T(8,128)(2,1)S(1)}, bf16[4,8,32,15]{3,1,2,0:T(8,128)(2,1)S(1)}, u32[]{:S(2)}, u32[]{:S(2)}) collective-permute-start(bf16[4,8,32,15]{3,1,2,0:T(8,128)(2,1)S(1)} %get-tuple-element.7), channel_id=1, source_target_pairs={{0,1},{1,2},{2,3},{3,4},{4,5},{5,6},{6,7},{7,8},{8,9},{9,10},{10,1... | collective-permute-start | bytes 92168 | tf_op jit(solution)/shard_map/ppermute | solution.py:23
  71.2 0.4 convolution_bitcast_fusion.11
  71.7 1.6 %collective-permute-done.3 = bf16[4,8,32,15]{3,1,2,0:T(8,128)(2,1)S(1)} collective-permute-done((bf16[4,8,32,15]{3,1,2,0:T(8,128)(2,1)S(1)}, bf16[4,8,32,15]{3,1,2,0:T(8,128)(2,1)S(1)}, u32[]{:S(2)}, u32[]{:S(2)}) %collective-permute-start.3) | collective-permute-done | bytes 30752 | tf_op jit(solution)/shard_map/ppermute | solution.py:25
  73.3 1.2 %collective-permute-done.2 = bf16[4,8,32,15]{3,1,2,0:T(8,128)(2,1)S(1)} collective-permute-done((bf16[4,8,32,15]{3,1,2,0:T(8,128)(2,1)S(1)}, bf16[4,8,32,15]{3,1,2,0:T(8,128)(2,1)S(1)}, u32[]{:S(2)}, u32[]{:S(2)}) %collective-permute-start.2) | collective-permute-done | bytes 30752 | tf_op jit(solution)/shard_map/ppermute | solution.py:23
  74.5 0.3 pad_maximum_fusion.8
  74.8 0.6 convolution_bitcast_fusion.6
  75.4 0.7 convolution_bitcast_fusion.5
  76.1 0.8 fusion.10
  77.1 1.9 %collective-permute-start.5 = (bf16[8,32,15]{2,1,0:T(8,128)(2,1)S(1)}, bf16[8,32,15]{2,1,0:T(8,128)(2,1)S(1)}, u32[]{:S(2)}, u32[]{:S(2)}) collective-permute-start(bf16[8,32,15]{2,1,0:T(8,128)(2,1)S(1)} %get-tuple-element.10), channel_id=1, source_target_pairs={{1,0},{2,1},{3,2},{4,3},{5,4},{6,5},{7,6},{8,7},{9,8},{10,9},{11,1... | collective-permute-start | bytes 23048 | tf_op jit(solution)/shard_map/ppermute | solution.py:25
  79.0 4.6 %collective-permute-start.4 = (bf16[8,32,15]{2,1,0:T(8,128)(2,1)S(1)}, bf16[8,32,15]{2,1,0:T(8,128)(2,1)S(1)}, u32[]{:S(2)}, u32[]{:S(2)}) collective-permute-start(bf16[8,32,15]{2,1,0:T(8,128)(2,1)S(1)} %get-tuple-element.9), channel_id=1, source_target_pairs={{0,1},{1,2},{2,3},{3,4},{4,5},{5,6},{6,7},{7,8},{8,9},{9,10},{10,1... | collective-permute-start | bytes 23048 | tf_op jit(solution)/shard_map/ppermute | solution.py:23
  83.6 1.1 %collective-permute-done.4 = bf16[8,32,15]{2,1,0:T(8,128)(2,1)S(1)} collective-permute-done((bf16[8,32,15]{2,1,0:T(8,128)(2,1)S(1)}, bf16[8,32,15]{2,1,0:T(8,128)(2,1)S(1)}, u32[]{:S(2)}, u32[]{:S(2)}) %collective-permute-start.4) | collective-permute-done | bytes 7712 | tf_op jit(solution)/shard_map/ppermute | solution.py:23
  84.7 0.4 convolution_bitcast_fusion
  85.2 0.7 convolution_bitcast_fusion.4
  85.9 0.9 fusion.9
  86.8 0.1 fusion.76
  86.9 1.9 %collective-permute-start.7 = (bf16[4,8,32,15]{3,1,2,0:T(8,128)(2,1)S(1)}, bf16[4,8,32,15]{3,1,2,0:T(8,128)(2,1)S(1)}, u32[]{:S(2)}, u32[]{:S(2)}) collective-permute-start(bf16[4,8,32,15]{3,1,2,0:T(8,128)(2,1)S(1)} %get-tuple-element.6), channel_id=1, source_target_pairs={{1,0},{2,1},{3,2},{4,3},{5,4},{6,5},{7,6},{8,7},{9,8},{10,9},{11,1... | collective-permute-start | bytes 92168 | tf_op jit(solution)/shard_map/ppermute | solution.py:25
  88.8 4.3 %collective-permute-start.6 = (bf16[4,8,32,15]{3,1,2,0:T(8,128)(2,1)S(1)}, bf16[4,8,32,15]{3,1,2,0:T(8,128)(2,1)S(1)}, u32[]{:S(2)}, u32[]{:S(2)}) collective-permute-start(bf16[4,8,32,15]{3,1,2,0:T(8,128)(2,1)S(1)} %get-tuple-element.5), channel_id=1, source_target_pairs={{0,1},{1,2},{2,3},{3,4},{4,5},{5,6},{6,7},{7,8},{8,9},{9,10},{10,1... | collective-permute-start | bytes 92168 | tf_op jit(solution)/shard_map/ppermute | solution.py:23
  93.1 2.1 %collective-permute-done.7 = bf16[4,8,32,15]{3,1,2,0:T(8,128)(2,1)S(1)} collective-permute-done((bf16[4,8,32,15]{3,1,2,0:T(8,128)(2,1)S(1)}, bf16[4,8,32,15]{3,1,2,0:T(8,128)(2,1)S(1)}, u32[]{:S(2)}, u32[]{:S(2)}) %collective-permute-start.7) | collective-permute-done | bytes 30752 | tf_op jit(solution)/shard_map/ppermute | solution.py:25
  95.2 1.9 %collective-permute-done.6 = bf16[4,8,32,15]{3,1,2,0:T(8,128)(2,1)S(1)} collective-permute-done((bf16[4,8,32,15]{3,1,2,0:T(8,128)(2,1)S(1)}, bf16[4,8,32,15]{3,1,2,0:T(8,128)(2,1)S(1)}, u32[]{:S(2)}, u32[]{:S(2)}) %collective-permute-start.6) | collective-permute-done | bytes 30752 | tf_op jit(solution)/shard_map/ppermute | solution.py:23
  97.1 0.3 pad_maximum_fusion.9
  97.5 0.6 convolution_bitcast_fusion.3
  98.0 0.7 convolution_bitcast_fusion.2
  98.8 0.8 fusion.11
  99.6 0.7 fusion.46
  (27 shorter events, 0.6 us)
Async XLA Ops:
  6.3 13.8 %copy-start = (f32[8,32,128]{2,1,0:T(8,128)S(1)}, f32[8,32,128]{2,1,0:T(8,128)}, u32[]{:S(2)}) copy-start(f32[8,32,128]{2,1,0:T(8,128)} %param.6) | copy-start | bytes 393220
  6.3 19.6 %copy-start.1 = (f32[1,4,3,31]{3,1,2,0:T(4,128)S(1)}, f32[1,4,3,31]{3,1,2,0:T(4,128)}, u32[]{:S(2)}) copy-start(f32[1,4,3,31]{3,1,2,0:T(4,128)} %param.7) | copy-start | bytes 4468
  6.3 40.3 %copy-start.3 = (s32[16]{0:T(128)S(1)}, s32[16]{0:T(128)}, u32[]{:S(2)}) copy-start(s32[16]{0:T(128)} %param.8) | copy-start | bytes 196
  6.3 43.1 %copy-start.2 = (s32[16,4]{0,1:T(4,128)S(1)}, s32[16,4]{0,1:T(4,128)}, u32[]{:S(2)}) copy-start(s32[16,4]{0,1:T(4,128)} %param.9) | copy-start | bytes 772
  12.8 39.9 %all-to-all-start = ((bf16[16,2,4096]{2,1,0:T(2,128)(2,1)}), bf16[16,2,4096]{2,1,0:T(2,128)(2,1)S(1)}, u32[]{:S(2)}, u32[]{:S(2)}) async-start(bf16[16,2,4096]{2,1,0:T(2,128)(2,1)} %reshape.127), calls=%async_computation | async-start | bytes 524288 | tf_op jit(solution)/shard_map/all_to_all | solution.py:75
  20.3 31.2 %collective-permute-start.1 = (bf16[8,32,15]{2,1,0:T(8,128)(2,1)S(1)}, bf16[8,32,15]{2,1,0:T(8,128)(2,1)S(1)}, u32[]{:S(2)}, u32[]{:S(2)}) collective-permute-start(bf16[8,32,15]{2,1,0:T(8,128)(2,1)S(1)} %get-tuple-element.12), channel_id=1, source_target_pairs={{1,0},{2,1},{3,2},{4,3},{5,4},{6,5},{7,6},{8,7},{9,8},{10,9},{11,1... | collective-permute-start | bytes 23048 | tf_op jit(solution)/shard_map/ppermute | solution.py:25
  22.3 29.2 %collective-permute-start = (bf16[8,32,15]{2,1,0:T(8,128)(2,1)S(1)}, bf16[8,32,15]{2,1,0:T(8,128)(2,1)S(1)}, u32[]{:S(2)}, u32[]{:S(2)}) collective-permute-start(bf16[8,32,15]{2,1,0:T(8,128)(2,1)S(1)} %get-tuple-element.11), channel_id=1, source_target_pairs={{0,1},{1,2},{2,3},{3,4},{4,5},{5,6},{6,7},{7,8},{8,9},{9,10},{10,1... | collective-permute-start | bytes 23048 | tf_op jit(solution)/shard_map/ppermute | solution.py:23
  65.6 7.7 %collective-permute-start.3 = (bf16[4,8,32,15]{3,1,2,0:T(8,128)(2,1)S(1)}, bf16[4,8,32,15]{3,1,2,0:T(8,128)(2,1)S(1)}, u32[]{:S(2)}, u32[]{:S(2)}) collective-permute-start(bf16[4,8,32,15]{3,1,2,0:T(8,128)(2,1)S(1)} %get-tuple-element.8), channel_id=1, source_target_pairs={{1,0},{2,1},{3,2},{4,3},{5,4},{6,5},{7,6},{8,7},{9,8},{10,9},{11,1... | collective-permute-start | bytes 92168 | tf_op jit(solution)/shard_map/ppermute | solution.py:25
  67.7 6.8 %collective-permute-start.2 = (bf16[4,8,32,15]{3,1,2,0:T(8,128)(2,1)S(1)}, bf16[4,8,32,15]{3,1,2,0:T(8,128)(2,1)S(1)}, u32[]{:S(2)}, u32[]{:S(2)}) collective-permute-start(bf16[4,8,32,15]{3,1,2,0:T(8,128)(2,1)S(1)} %get-tuple-element.7), channel_id=1, source_target_pairs={{0,1},{1,2},{2,3},{3,4},{4,5},{5,6},{6,7},{7,8},{8,9},{9,10},{10,1... | collective-permute-start | bytes 92168 | tf_op jit(solution)/shard_map/ppermute | solution.py:23
  77.1 6.5 %collective-permute-start.5 = (bf16[8,32,15]{2,1,0:T(8,128)(2,1)S(1)}, bf16[8,32,15]{2,1,0:T(8,128)(2,1)S(1)}, u32[]{:S(2)}, u32[]{:S(2)}) collective-permute-start(bf16[8,32,15]{2,1,0:T(8,128)(2,1)S(1)} %get-tuple-element.10), channel_id=1, source_target_pairs={{1,0},{2,1},{3,2},{4,3},{5,4},{6,5},{7,6},{8,7},{9,8},{10,9},{11,1... | collective-permute-start | bytes 23048 | tf_op jit(solution)/shard_map/ppermute | solution.py:25
  79.0 5.7 %collective-permute-start.4 = (bf16[8,32,15]{2,1,0:T(8,128)(2,1)S(1)}, bf16[8,32,15]{2,1,0:T(8,128)(2,1)S(1)}, u32[]{:S(2)}, u32[]{:S(2)}) collective-permute-start(bf16[8,32,15]{2,1,0:T(8,128)(2,1)S(1)} %get-tuple-element.9), channel_id=1, source_target_pairs={{0,1},{1,2},{2,3},{3,4},{4,5},{5,6},{6,7},{7,8},{8,9},{9,10},{10,1... | collective-permute-start | bytes 23048 | tf_op jit(solution)/shard_map/ppermute | solution.py:23
  86.9 8.3 %collective-permute-start.7 = (bf16[4,8,32,15]{3,1,2,0:T(8,128)(2,1)S(1)}, bf16[4,8,32,15]{3,1,2,0:T(8,128)(2,1)S(1)}, u32[]{:S(2)}, u32[]{:S(2)}) collective-permute-start(bf16[4,8,32,15]{3,1,2,0:T(8,128)(2,1)S(1)} %get-tuple-element.6), channel_id=1, source_target_pairs={{1,0},{2,1},{3,2},{4,3},{5,4},{6,5},{7,6},{8,7},{9,8},{10,9},{11,1... | collective-permute-start | bytes 92168 | tf_op jit(solution)/shard_map/ppermute | solution.py:25
  88.8 8.3 %collective-permute-start.6 = (bf16[4,8,32,15]{3,1,2,0:T(8,128)(2,1)S(1)}, bf16[4,8,32,15]{3,1,2,0:T(8,128)(2,1)S(1)}, u32[]{:S(2)}, u32[]{:S(2)}) collective-permute-start(bf16[4,8,32,15]{3,1,2,0:T(8,128)(2,1)S(1)} %get-tuple-element.5), channel_id=1, source_target_pairs={{0,1},{1,2},{2,3},{3,4},{4,5},{5,6},{6,7},{7,8},{8,9},{9,10},{10,1... | collective-permute-start | bytes 92168 | tf_op jit(solution)/shard_map/ppermute | solution.py:23
where the time goes:
time: 101 us; the launch traced here: 100 us
  starting transfers between devices  31.2 us (31%)
  local copies, waits for them, and re-layouts  25.6 us (25%)
  blocking collectives  20.7 us (20%)
  matrix products  12.2 us (12%)
  waiting for transfers between devices  7.98 us (8%)
  other arithmetic  2.37 us (2%)
    all_gather x1, blocking collectives, shards(): fitted = lax.all_gather(psf_bank, ('plane', 'brick'), axis=0, tiled=True)  20.7 us
    unnamed x11, local copies, waits for them, and re-layouts  18.8 us
    ppermute x4, starting transfers between devices, padded_2(): lax.ppermute(tail, axis, [(i, (i + 1) % count) for i in range(ends)])  15.9 us
    ppermute x4, starting transfers between devices, padded_2(): lax.ppermute(head, axis, [((i + 1) % count, i) for i in range(ends)])  7.93 us
    all_to_all x1, starting transfers between devices, shards(): lax.all_to_all(camera_rows, ('plane', 'brick'), split_axis=3, concat_axis...  7.35 us
    convert_element_type x1, local copies, waits for them, and re-layouts, shards(): regrouped.astype(jnp.float32) / (blurred + BACKGROUND)  5.93 us
    ppermute x4, waiting for transfers between devices, padded_2(): lax.ppermute(tail, axis, [(i, (i + 1) % count) for i in range(ends)])  4.22 us
    ppermute x4, waiting for transfers between devices, padded_2(): lax.ppermute(head, axis, [((i + 1) % count, i) for i in range(ends)])  3.76 us
  transfers between devices with their start and end apart: 9, of which 5 were waited for; matrix products, arithmetic and copies ran while one was open for 7% of the time, Pallas kernels for 0%

commit v1 on v0

--- a/solution.py
+++ b/solution.py
@@ -1,17 +1,22 @@
+import functools
+
 import jax
 import jax.numpy as jnp
 from jax import lax
+from jax.experimental import pallas as pl
+from jax.experimental.pallas import tpu as pltpu
 from jax.sharding import PartitionSpec as P
 
 V = 4
 RADIUS = 15
 ITERS = 2
+EDGE = 16
 
 
 BACKGROUND = 0.1
 HIGHEST = lax.Precision.HIGHEST
-
-
+F32 = jnp.float32
+BF16 = jnp.bfloat16
 def padded_2(cells, sides, width):
     for axis, dim in sides:
         count = lax.axis_size(axis)
@@ -119,9 +124,319 @@
     return current
 
 
+def split(a):
+    hi = a.astype(BF16)
+    return hi, (a - hi.astype(F32)).astype(BF16)
+
+
+def dot(a, b, nt=False):
+    dims = (((1,), (1 if nt else 0,)), ((), ()))
+    return lax.dot_general(a, b, dims, preferred_element_type=F32)
+
+
+def dot3(a, b, nt=False):
+    return dot(a[0], b[0], nt) + (dot(a[0], b[1], nt) + dot(a[1], b[0], nt))
+
+
+def dot2(a, b, nt=False):
+    return dot(a, b[0], nt) + dot(a, b[1], nt)
+
+
+def exact(a, b):
+    return lax.dot_general(a, b, (((1,), (0,)), ((), ())), precision=HIGHEST, preferred_element_type=F32)
+
+
+def fused(
+    dims, cam, est, psf, owner, mask, out,
+    taps, gath, camrecv, camt, xsend, xhalo, rsend, rhalo, kbh, kbl, abl, aback, xt,
+    psf_sems, cam_sems, x_sems, r_sems, own_sem,
+):
+    n, brick, zd, rows, cols = dims
+    lr = rows // n
+    part = zd * lr
+    cells = zd * rows
+    taps_n = psf.shape[-1]
+    me = lax.axis_index("plane") * brick + lax.axis_index("brick")
+
+    def device(t):
+        return {"plane": lax.div(t, brick), "brick": lax.rem(t, brick)}
+
+    def peer(k):
+        return lax.rem(me + k, n)
+
+    barrier = pltpu.get_barrier_semaphore()
+    for k in range(1, n):
+        pl.semaphore_signal(barrier, inc=1, device_id=device(peer(k)), device_id_type=pl.DeviceIdType.MESH)
+
+    has_left = me > 0
+    has_right = me < n - 1
+    zero_edge = jnp.zeros((EDGE, cells), BF16)
+
+    @pl.when(me == 0)
+    def _():
+        for it in range(ITERS):
+            xhalo[it, 0:EDGE, :] = zero_edge
+            for v in range(V):
+                rhalo[it, v, 0:EDGE, :] = zero_edge
+
+    @pl.when(me == n - 1)
+    def _():
+        for it in range(ITERS):
+            xhalo[it, EDGE:, :] = zero_edge
+            for v in range(V):
+                rhalo[it, v, EDGE:, :] = zero_edge
+
+    def x_copy(it, side):
+        rows_of = pl.ds(side * EDGE, EDGE)
+        return pltpu.make_async_remote_copy(
+            src_ref=xsend.at[it, rows_of], dst_ref=xhalo.at[it, rows_of],
+            send_sem=x_sems.at[0, it, side], recv_sem=x_sems.at[1, it, side],
+            device_id=device(lax.rem(me + n + 1 - 2 * side, n)), device_id_type=pl.DeviceIdType.MESH,
+        )
+
+    def r_copy(it, side):
+        rows_of = pl.ds(side * EDGE, EDGE)
+        return pltpu.make_async_remote_copy(
+            src_ref=rsend.at[it, :, rows_of], dst_ref=rhalo.at[it, :, rows_of],
+            send_sem=r_sems.at[0, it, side], recv_sem=r_sems.at[1, it, side],
+            device_id=device(lax.rem(me + n + 1 - 2 * side, n)), device_id_type=pl.DeviceIdType.MESH,
+        )
+
+    def start(make, it):
+        @pl.when(has_right)
+        def _():
+            make(it, 0).start()
+
+        @pl.when(has_left)
+        def _():
+            make(it, 1).start()
+
+    def arrive(make, it):
+        @pl.when(has_left)
+        def _():
+            make(it, 0).wait_recv()
+
+        @pl.when(has_right)
+        def _():
+            make(it, 1).wait_recv()
+
+    def finish(make, it):
+        @pl.when(has_right)
+        def _():
+            make(it, 0).wait_send()
+
+        @pl.when(has_left)
+        def _():
+            make(it, 1).wait_send()
+
+    def psf_copy(k):
+        return pltpu.make_async_remote_copy(
+            src_ref=psf.at[0], dst_ref=gath.at[me],
+            send_sem=psf_sems.at[0, k], recv_sem=psf_sems.at[1, k],
+            device_id=device(peer(k)), device_id_type=pl.DeviceIdType.MESH,
+        )
+
+    def cam_copy(k):
+        return pltpu.make_async_remote_copy(
+            src_ref=cam.at[:, pl.ds(pl.multiple_of(peer(k) * cols, cols), cols)], dst_ref=camrecv.at[me],
+            send_sem=cam_sems.at[0, k], recv_sem=cam_sems.at[1, k],
+            device_id=device(peer(k)), device_id_type=pl.DeviceIdType.MESH,
+        )
+
+    own = pltpu.make_async_copy(
+        cam.at[:, pl.ds(pl.multiple_of(me * cols, cols), cols)], camrecv.at[me], own_sem
+    )
+    own.start()
+    x0 = est[...].T
+    xt[...] = x0
+    xsend[0, 0:EDGE, :] = x0[cols - EDGE :, :].astype(BF16)
+    xsend[0, EDGE:, :] = x0[:EDGE, :].astype(BF16)
+    gath[me] = psf[0]
+
+    pl.semaphore_wait(barrier, n - 1)
+    for k in range(1, n):
+        psf_copy(k).start()
+    start(x_copy, 0)
+    for k in range(1, n):
+        cam_copy(k).start()
+
+    lane = lax.broadcasted_iota(jnp.int32, (128, cells), 1)
+    line = lax.broadcasted_iota(jnp.int32, (128, cells), 0)
+    y_of = lax.shift_right_logical(lane, part.bit_length() - 1) * lr + (lane & (lr - 1))
+    z_of = lax.shift_right_logical(lane, lr.bit_length() - 1) & (zd - 1)
+    pick_y = (y_of == line).astype(F32)
+    pick_z = (z_of == line).astype(F32)
+    flip = (
+        lax.broadcasted_iota(jnp.int32, (128, 128), 0) + lax.broadcasted_iota(jnp.int32, (128, 128), 1)
+        == taps_n - 1
+    ).astype(F32)
+    taps[...] = jnp.zeros_like(taps)
+
+    for k in range(1, n):
+        psf_copy(k).wait_recv()
+    block = gath[owner[me]]
+    for a in range(3):
+        for v in range(V):
+            taps[pl.ds(a * V + v, 1), 0:taps_n] = block[v, a : a + 1, :]
+    kernels = taps[...]
+    total = jnp.sum(kernels, axis=-1, keepdims=True)
+    kernels = kernels / jnp.where(total > 0.0, total, 1.0)
+    flipped = exact(kernels, flip)
+
+    def toeplitz(row, height, width):
+        if width > 128:
+            row = jnp.concatenate([row, jnp.zeros((1, width - 128), F32)], axis=1)
+        return pltpu.roll(
+            jnp.broadcast_to(row, (height, width)), width - RADIUS, 1, stride=1, stride_axis=0
+        )
+
+    lines_y = jnp.concatenate([toeplitz(flipped[V + v : V + v + 1], rows, 128) for v in range(V)], axis=0)
+    lines_z = jnp.concatenate([toeplitz(flipped[v : v + 1], zd, 128) for v in range(V)], axis=0)
+    wide_y = exact(lines_y, pick_y)
+    wide_z = exact(lines_z, pick_z)
+    seen = [mask[me, v] > 0 for v in range(V)]
+    back_edge = jnp.zeros((cols, 128), F32)
+    for v in range(V):
+        for z in range(zd):
+            piece = wide_y[v * rows : (v + 1) * rows] * wide_z[v * zd + z : v * zd + z + 1]
+            hi, lo = split(piece)
+            kbh[v, z * rows : (z + 1) * rows, :] = hi
+            kbl[v, z * rows : (z + 1) * rows, :] = lo
+        band = toeplitz(kernels[2 * V + v : 2 * V + v + 1], cols, 2 * cols)
+        hi, lo = split(band[:, :cols])
+        abl[0, v] = hi
+        abl[1, v] = lo
+        hi, lo = split(pltpu.roll(band[:, cols:], EDGE, 1))
+        abl[2, v] = hi
+        abl[3, v] = lo
+        band = jnp.where(seen[v], toeplitz(flipped[2 * V + v : 2 * V + v + 1], cols, 2 * cols), 0.0)
+        hi, lo = split(band[:, :cols])
+        aback[0, v] = hi
+        aback[1, v] = lo
+        back_edge = back_edge + pltpu.roll(band[:, cols:], (EDGE + 2 * EDGE * v) % 128, 1)
+    back_edge = split(back_edge)
+    unseen = functools.reduce(jnp.add, [jnp.where(s, 0.0, 1.0) for s in seen])
+
+    for it in range(ITERS):
+        x = split(xt[...])
+        blurred = []
+        for v in range(V):
+            spread = split(dot3(x, (kbh[v], kbl[v])))
+            blurred.append(dot3((abl[0, v], abl[1, v]), spread))
+        arrive(x_copy, it)
+        edge = xhalo[it]
+        for v in range(V):
+            spread = split(dot2(edge, (kbh[v], kbl[v])))
+            blurred[v] = blurred[v] + dot3((abl[2, v, :, 0 : 2 * EDGE], abl[3, v, :, 0 : 2 * EDGE]), spread)
+        if it == 0:
+            for k in range(1, n):
+                cam_copy(k).wait_recv()
+            own.wait()
+            for v in range(V):
+                tile = camrecv[:, v * part : (v + 1) * part, :].reshape(cells, cols)
+                camt[v] = tile.astype(F32).T
+        ratios = []
+        for v in range(V):
+            ratio = jnp.where(seen[v], camt[v] / (blurred[v] + BACKGROUND), 0.0)
+            rsend[it, v, 0:EDGE, :] = ratio[cols - EDGE :, :].astype(BF16)
+            rsend[it, v, EDGE:, :] = ratio[:EDGE, :].astype(BF16)
+            ratios.append(ratio)
+        start(r_copy, it)
+        total = jnp.zeros((cols, cells), F32)
+        for v in range(V):
+            spread = split(dot3(split(ratios[v]), (kbh[v], kbl[v]), nt=True))
+            total = total + dot3((aback[0, v], aback[1, v]), spread)
+        arrive(r_copy, it)
+        spread = [dot2(rhalo[it, v], (kbh[v], kbl[v]), nt=True) for v in range(V)]
+        total = total + dot3(back_edge, split(jnp.concatenate(spread, axis=0)))
+        fresh = xt[...] * ((total + unseen) * (1.0 / V))
+        if it < ITERS - 1:
+            xsend[it + 1, 0:EDGE, :] = fresh[cols - EDGE :, :].astype(BF16)
+            xsend[it + 1, EDGE:, :] = fresh[:EDGE, :].astype(BF16)
+            start(x_copy, it + 1)
+            xt[...] = fresh
+        else:
+            out[...] = fresh.T
+
+    for k in range(1, n):
+        psf_copy(k).wait_send()
+        cam_copy(k).wait_send()
+    for it in range(ITERS):
+        finish(x_copy, it)
+        finish(r_copy, it)
+
+
+def power_of_two(a):
+    return a & (a - 1) == 0
+
+
+def fused_shards(dims, camera_rows, estimate, psf_bank, psf_owner, view_mask):
+    n, brick, zd, rows, cols = dims
+    lr = rows // n
+    cells = zd * rows
+    vmem = pl.BlockSpec(memory_space=pltpu.VMEM)
+    smem = pl.BlockSpec(memory_space=pltpu.SMEM)
+    result = pl.pallas_call(
+        functools.partial(fused, dims),
+        out_shape=jax.ShapeDtypeStruct((cells, cols), F32),
+        in_specs=[vmem, vmem, vmem, smem, smem],
+        out_specs=vmem,
+        scratch_shapes=[
+            pltpu.VMEM((16, 128), F32),
+            pltpu.VMEM((n,) + psf_bank.shape[1:], F32),
+            pltpu.VMEM((n, V * zd * lr, cols), BF16),
+            pltpu.VMEM((V, cols, cells), F32),
+            pltpu.VMEM((ITERS, 2 * EDGE, cells), BF16),
+            pltpu.VMEM((ITERS, 2 * EDGE, cells), BF16),
+            pltpu.VMEM((ITERS, V, 2 * EDGE, cells), BF16),
+            pltpu.VMEM((ITERS, V, 2 * EDGE, cells), BF16),
+            pltpu.VMEM((V, cells, cells), BF16),
+            pltpu.VMEM((V, cells, cells), BF16),
+            pltpu.VMEM((4, V, cols, cols), BF16),
+            pltpu.VMEM((2, V, cols, cols), BF16),
+            pltpu.VMEM((cols, cells), F32),
+            pltpu.SemaphoreType.DMA((2, n)),
+            pltpu.SemaphoreType.DMA((2, n)),
+            pltpu.SemaphoreType.DMA((2, ITERS, 2)),
+            pltpu.SemaphoreType.DMA((2, ITERS, 2)),
+            pltpu.SemaphoreType.DMA,
+        ],
+        compiler_params=pltpu.CompilerParams(
+            collective_id=0, has_side_effects=True, vmem_limit_bytes=32 * 1024 * 1024
+        ),
+    )(
+        camera_rows.reshape(V * zd * lr, n * cols),
+        estimate.reshape(cells, cols),
+        psf_bank,
+        psf_owner,
+        view_mask,
+    )
+    return result.reshape(zd, rows, cols)
+
+
 def solution(mesh):
+    n = mesh.shape["plane"] * mesh.shape["brick"]
+
+    def shards_of(camera_rows, estimate, psf_bank, psf_owner, view_mask):
+        zd, rows, cols = estimate.shape
+        lr = camera_rows.shape[2]
+        small = (
+            zd * rows == 256
+            and cols == 128
+            and psf_bank.shape[-1] == 2 * RADIUS + 1
+            and lr * n == rows
+            and zd % 8 == 0
+            and zd * lr % 16 == 0
+            and power_of_two(zd)
+            and power_of_two(lr)
+        )
+        if not small:
+            return shards(camera_rows, estimate, psf_bank, psf_owner, view_mask)
+        dims = (n, mesh.shape["brick"], zd, rows, cols)
+        return fused_shards(dims, camera_rows, estimate, psf_bank, psf_owner, view_mask)
+
     return jax.shard_map(
-        shards,
+        shards_of,
         mesh=mesh,
         in_specs=(
             P(None, "slab", ("plane", "brick"), None),

time: 101 us -> 28.2 us (0.28)
  starting transfers between devices: 31.2 us -> 0 us
  Pallas kernels: 0 us -> 25.4 us
  local copies, waits for them, and re-layouts: 25.6 us -> 2.54 us
  blocking collectives: 20.7 us -> 0 us
  matrix products: 12.2 us -> 0 us
  waiting for transfers between devices: 7.98 us -> 0 us
  other arithmetic: 2.37 us -> 0 us
    pallas_call x0 -> x1, Pallas kernels: none -> 25.4 us  [fused_shards(): pl.pallas_call(functools.partial(fused, dims), out_shape=jax.ShapeDtypeSt...]
    ppermute x8 -> x0, starting transfers between devices: 23.8 us -> none  [the longest x4 15.9 us: padded_2(): lax.ppermute(tail, axis, [(i, (i + 1) % count) for i in range(ends)])]
    all_gather x1 -> x0, blocking collectives: 20.7 us -> none  [shards(): fitted = lax.all_gather(psf_bank, ('plane', 'brick'), axis=0, tiled=True)]
    unnamed x11 -> x9, local copies, waits for them, and re-layouts: 18.8 us -> 1.46 us
    dot_general x19 -> x0, matrix products: 12.2 us -> none  [the longest x4 3.37 us: across_depth(): return jnp.einsum('vzyc,vzw->vwyc', volume, band_z, precision=HIGHEST)]
    ppermute x8 -> x0, waiting for transfers between devices: 7.97 us -> none  [the longest x4 4.22 us: padded_2(): lax.ppermute(tail, axis, [(i, (i + 1) % count) for i in range(ends)])]
    all_to_all x1 -> x0, starting transfers between devices: 7.35 us -> none  [shards(): lax.all_to_all(camera_rows, ('plane', 'brick'), split_axis=3, concat_axis...]
    convert_element_type x1 -> x0, local copies, waits for them, and re-layouts: 5.93 us -> none  [shards(): regrouped.astype(jnp.float32) / (blurred + BACKGROUND)]
  transfers between devices with their start and end apart: 9 -> 0, of which waited for: 5 -> 0; matrix products, arithmetic and copies ran while one was open for 7% -> 0% of each run, Pallas kernels for 0% -> 0%
where the time goes in v1:
time: 28.2 us; the launch traced here: 28 us
  Pallas kernels  25.4 us (90%)
  local copies, waits for them, and re-layouts  2.54 us (9%)
    pallas_call x1, Pallas kernels, fused_shards(): pl.pallas_call(functools.partial(fused, dims), out_shape=jax.ShapeDtypeSt...  25.4 us
    unnamed x9, local copies, waits for them, and re-layouts  1.46 us
    reshape x1, local copies, waits for them, and re-layouts, fused_shards(): camera_rows.reshape(V * zd * lr, n * cols)  1.08 us

profile of v1, /device:TPU:1, one launch (start us, length us, event | category | flops | bytes accessed | tf_op | source)
XLA Modules:
  0.0 28.0 jit_solution(4524440553709574801)
XLA Ops:
  0.0 0.0 copy-start.2
  0.0 0.7 %copy.6.psf = f32[1,4,3,31]{3,2,1,0:T(4,128)S(1)} copy(f32[1,4,3,31]{3,1,2,0:T(4,128)} %param.7) | data formatting | bytes 2976 | tf_op args[2]
  0.7 0.0 copy-done.2
  0.7 0.1 copy.7.mask
  0.8 0.0 copy-start
  0.8 0.0 copy-start.1
  0.8 1.1 %reshape.9.cam = bf16[64,2048]{1,0:T(8,128)(2,1)S(1)} reshape(bf16[4,8,2,2048]{3,2,1,0:T(2,128)(2,1)} %param.5) | data formatting | bytes 524288 | tf_op jit(solution)/shard_map/reshape | solution.py:408
  1.9 0.0 copy-done
  1.9 0.0 copy-done.1
  1.9 25.4 %shard_map.55 = f32[256,128]{1,0:T(8,128)S(1)} custom-call(bf16[64,2048]{1,0:T(8,128)(2,1)S(1)} %reshape.9.cam, f32[256,128]{1,0:T(8,128)S(1)} %bitcast.3, f32[1,4,3,31]{3,2,1,0:T(4,128)S(1)} %copy.6.psf, s32[16]{0:T(128)S(1)} %copy-done.1, s32[16,4]{1,0:T(8,128)S(1)} %copy.7.mask), custom_call_target="tpu_custom_call" | custom-call | tf_op jit(solution)/shard_map/pallas_call | solution.py:379
  27.3 0.7 %copy.9 = f32[8,32,128]{2,1,0:T(8,128)} copy(f32[8,32,128]{2,1,0:T(8,128)S(1)} %bitcast.2) | data formatting | bytes 262144
Async XLA Ops:
  0.0 0.7 %copy-start.2 = (s32[16,4]{0,1:T(4,128)S(1)}, s32[16,4]{0,1:T(4,128)}, u32[]{:S(2)}) copy-start(s32[16,4]{0,1:T(4,128)} %param.9) | copy-start | bytes 772
  0.8 1.1 %copy-start = (f32[8,32,128]{2,1,0:T(8,128)S(1)}, f32[8,32,128]{2,1,0:T(8,128)}, u32[]{:S(2)}) copy-start(f32[8,32,128]{2,1,0:T(8,128)} %param.6) | copy-start | bytes 393220
  0.8 1.1 %copy-start.1 = (s32[16]{0:T(128)S(1)}, s32[16]{0:T(128)}, u32[]{:S(2)}) copy-start(s32[16]{0:T(128)} %owner.1) | copy-start | bytes 196

commit v2 on v1

--- a/solution.py
+++ b/solution.py
@@ -254,10 +254,11 @@
     gath[me] = psf[0]
 
     pl.semaphore_wait(barrier, n - 1)
-    for k in range(1, n):
+    far_first = sorted(range(1, n), key=lambda k: -min(k, n - k))
+    for k in far_first:
         psf_copy(k).start()
     start(x_copy, 0)
-    for k in range(1, n):
+    for k in far_first:
         cam_copy(k).start()
 
     lane = lax.broadcasted_iota(jnp.int32, (128, cells), 1)
@@ -276,8 +277,7 @@
         psf_copy(k).wait_recv()
     block = gath[owner[me]]
     for a in range(3):
-        for v in range(V):
-            taps[pl.ds(a * V + v, 1), 0:taps_n] = block[v, a : a + 1, :]
+        taps[a * V : (a + 1) * V, 0:taps_n] = block[a]
     kernels = taps[...]
     total = jnp.sum(kernels, axis=-1, keepdims=True)
     kernels = kernels / jnp.where(total > 0.0, total, 1.0)
@@ -294,7 +294,7 @@
     lines_z = jnp.concatenate([toeplitz(flipped[v : v + 1], zd, 128) for v in range(V)], axis=0)
     wide_y = exact(lines_y, pick_y)
     wide_z = exact(lines_z, pick_z)
-    seen = [mask[me, v] > 0 for v in range(V)]
+    seen = [mask[v, me] > 0 for v in range(V)]
     back_edge = jnp.zeros((cols, 128), F32)
     for v in range(V):
         for z in range(zd):
@@ -383,7 +383,7 @@
         out_specs=vmem,
         scratch_shapes=[
             pltpu.VMEM((16, 128), F32),
-            pltpu.VMEM((n,) + psf_bank.shape[1:], F32),
+            pltpu.VMEM((n, 3, V, psf_bank.shape[-1]), F32),
             pltpu.VMEM((n, V * zd * lr, cols), BF16),
             pltpu.VMEM((V, cols, cells), F32),
             pltpu.VMEM((ITERS, 2 * EDGE, cells), BF16),
@@ -407,9 +407,9 @@
     )(
         camera_rows.reshape(V * zd * lr, n * cols),
         estimate.reshape(cells, cols),
-        psf_bank,
+        psf_bank.transpose(0, 2, 1, 3),
         psf_owner,
-        view_mask,
+        view_mask.T,
     )
     return result.reshape(zd, rows, cols)
 

time: 28.2 us -> 27.8 us (0.986)
  the two profiles are of different devices: /device:TPU:1 before, /device:TPU:13 now
where the time goes in v2:
time: 27.8 us; the launch traced here: 27.6 us
  Pallas kernels  25.8 us (93%)
  local copies, waits for them, and re-layouts  1.76 us (6%)
    pallas_call x1, Pallas kernels, fused_shards(): pl.pallas_call(functools.partial(fused, dims), out_shape=jax.ShapeDtypeSt...  25.8 us
    reshape x1, local copies, waits for them, and re-layouts, fused_shards(): camera_rows.reshape(V * zd * lr, n * cols)  1.08 us
    unnamed x9, local copies, waits for them, and re-layouts  0.67 us

profile of v2, /device:TPU:13, one launch (start us, length us, event | category | flops | bytes accessed | tf_op | source)
XLA Modules:
  0.0 27.6 jit_solution(14444365695401966927)
XLA Ops:
  0.0 0.0 copy-start
  0.0 0.0 copy-start.1
  0.0 0.0 copy-start.2
  0.0 0.0 copy-start.3
  0.0 1.1 %reshape.9.cam = bf16[64,2048]{1,0:T(8,128)(2,1)S(1)} reshape(bf16[4,8,2,2048]{3,2,1,0:T(2,128)(2,1)} %param.5) | data formatting | bytes 524288 | tf_op jit(solution)/shard_map/reshape | solution.py:408
  1.1 0.0 copy-done
  1.1 0.0 copy-done.1
  1.1 0.0 copy-done.2
  1.1 0.0 copy-done.3
  1.1 25.8 %shard_map.55 = f32[256,128]{1,0:T(8,128)S(1)} custom-call(bf16[64,2048]{1,0:T(8,128)(2,1)S(1)} %reshape.9.cam, f32[256,128]{1,0:T(8,128)S(1)} %bitcast.5, f32[1,3,4,31]{3,2,1,0:T(4,128)S(1)} %bitcast.6, s32[16]{0:T(128)S(1)} %copy-done.3, s32[4,16]{1,0:T(4,128)S(1)} %bitcast.7), custom_call_target="tpu_custom_call" | custom-call | tf_op jit(solution)/shard_map/pallas_call | solution.py:379
  27.0 0.7 %copy.7 = f32[8,32,128]{2,1,0:T(8,128)} copy(f32[8,32,128]{2,1,0:T(8,128)S(1)} %bitcast.4) | data formatting | bytes 262144
Async XLA Ops:
  0.0 1.1 %copy-start = (f32[8,32,128]{2,1,0:T(8,128)S(1)}, f32[8,32,128]{2,1,0:T(8,128)}, u32[]{:S(2)}) copy-start(f32[8,32,128]{2,1,0:T(8,128)} %param.6) | copy-start | bytes 393220
  0.0 1.1 %copy-start.1 = (f32[1,4,3,31]{3,1,2,0:T(4,128)S(1)}, f32[1,4,3,31]{3,1,2,0:T(4,128)}, u32[]{:S(2)}) copy-start(f32[1,4,3,31]{3,1,2,0:T(4,128)} %param.7) | copy-start | bytes 4468
  0.0 1.1 %copy-start.2 = (s32[16,4]{0,1:T(4,128)S(1)}, s32[16,4]{0,1:T(4,128)}, u32[]{:S(2)}) copy-start(s32[16,4]{0,1:T(4,128)} %param.9) | copy-start | bytes 772
  0.0 1.1 %copy-start.3 = (s32[16]{0:T(128)S(1)}, s32[16]{0:T(128)}, u32[]{:S(2)}) copy-start(s32[16]{0:T(128)} %owner.1) | copy-start | bytes 196

commit v3 on v2

--- a/solution.py
+++ b/solution.py
@@ -254,7 +254,7 @@
     gath[me] = psf[0]
 
     pl.semaphore_wait(barrier, n - 1)
-    far_first = sorted(range(1, n), key=lambda k: -min(k, n - k))
+    far_first = list(range(1, n))
     for k in far_first:
         psf_copy(k).start()
     start(x_copy, 0)
@@ -311,8 +311,8 @@
         abl[3, v] = lo
         band = jnp.where(seen[v], toeplitz(flipped[2 * V + v : 2 * V + v + 1], cols, 2 * cols), 0.0)
         hi, lo = split(band[:, :cols])
-        aback[0, v] = hi
-        aback[1, v] = lo
+        aback[0, :, v * cols : (v + 1) * cols] = hi
+        aback[1, :, v * cols : (v + 1) * cols] = lo
         back_edge = back_edge + pltpu.roll(band[:, cols:], (EDGE + 2 * EDGE * v) % 128, 1)
     back_edge = split(back_edge)
     unseen = functools.reduce(jnp.add, [jnp.where(s, 0.0, 1.0) for s in seen])
@@ -342,10 +342,10 @@
             rsend[it, v, EDGE:, :] = ratio[:EDGE, :].astype(BF16)
             ratios.append(ratio)
         start(r_copy, it)
-        total = jnp.zeros((cols, cells), F32)
-        for v in range(V):
-            spread = split(dot3(split(ratios[v]), (kbh[v], kbl[v]), nt=True))
-            total = total + dot3((aback[0, v], aback[1, v]), spread)
+        spread = [split(dot3(split(ratios[v]), (kbh[v], kbl[v]), nt=True)) for v in range(V)]
+        hi = jnp.concatenate([a for a, _ in spread], axis=0)
+        lo = jnp.concatenate([b for _, b in spread], axis=0)
+        total = dot3((aback[0], aback[1]), (hi, lo))
         arrive(r_copy, it)
         spread = [dot2(rhalo[it, v], (kbh[v], kbl[v]), nt=True) for v in range(V)]
         total = total + dot3(back_edge, split(jnp.concatenate(spread, axis=0)))
@@ -393,7 +393,7 @@
             pltpu.VMEM((V, cells, cells), BF16),
             pltpu.VMEM((V, cells, cells), BF16),
             pltpu.VMEM((4, V, cols, cols), BF16),
-            pltpu.VMEM((2, V, cols, cols), BF16),
+            pltpu.VMEM((2, cols, V * cols), BF16),
             pltpu.VMEM((cols, cells), F32),
             pltpu.SemaphoreType.DMA((2, n)),
             pltpu.SemaphoreType.DMA((2, n)),

time: 27.8 us -> 27 us (0.971)
  the two profiles are of different devices: /device:TPU:13 before, /device:TPU:1 now
where the time goes in v3:
time: 27 us; the launch traced here: 26.9 us
  Pallas kernels  25.1 us (93%)
  local copies, waits for them, and re-layouts  1.76 us (7%)
    pallas_call x1, Pallas kernels, fused_shards(): pl.pallas_call(functools.partial(fused, dims), out_shape=jax.ShapeDtypeSt...  25.1 us
    reshape x1, local copies, waits for them, and re-layouts, fused_shards(): camera_rows.reshape(V * zd * lr, n * cols)  1.08 us
    unnamed x9, local copies, waits for them, and re-layouts  0.67 us

profile of v3, /device:TPU:1, one launch (start us, length us, event | category | flops | bytes accessed | tf_op | source)
XLA Modules:
  0.0 26.9 jit_solution(10502455447401688707)
XLA Ops:
  0.0 0.0 copy-start
  0.0 0.0 copy-start.1
  0.0 0.0 copy-start.2
  0.0 0.0 copy-start.3
  0.0 1.1 %reshape.9.cam = bf16[64,2048]{1,0:T(8,128)(2,1)S(1)} reshape(bf16[4,8,2,2048]{3,2,1,0:T(2,128)(2,1)} %param.5) | data formatting | bytes 524288 | tf_op jit(solution)/shard_map/reshape | solution.py:408
  1.1 0.0 copy-done
  1.1 0.0 copy-done.1
  1.1 0.0 copy-done.2
  1.1 0.0 copy-done.3
  1.1 25.1 %shard_map.55 = f32[256,128]{1,0:T(8,128)S(1)} custom-call(bf16[64,2048]{1,0:T(8,128)(2,1)S(1)} %reshape.9.cam, f32[256,128]{1,0:T(8,128)S(1)} %bitcast.5, f32[1,3,4,31]{3,2,1,0:T(4,128)S(1)} %bitcast.6, s32[16]{0:T(128)S(1)} %copy-done.3, s32[4,16]{1,0:T(4,128)S(1)} %bitcast.7), custom_call_target="tpu_custom_call" | custom-call | tf_op jit(solution)/shard_map/pallas_call | solution.py:379
  26.2 0.7 %copy.7 = f32[8,32,128]{2,1,0:T(8,128)} copy(f32[8,32,128]{2,1,0:T(8,128)S(1)} %bitcast.4) | data formatting | bytes 262144
Async XLA Ops:
  0.0 1.1 %copy-start = (f32[8,32,128]{2,1,0:T(8,128)S(1)}, f32[8,32,128]{2,1,0:T(8,128)}, u32[]{:S(2)}) copy-start(f32[8,32,128]{2,1,0:T(8,128)} %param.6) | copy-start | bytes 393220
  0.0 1.1 %copy-start.1 = (f32[1,4,3,31]{3,1,2,0:T(4,128)S(1)}, f32[1,4,3,31]{3,1,2,0:T(4,128)}, u32[]{:S(2)}) copy-start(f32[1,4,3,31]{3,1,2,0:T(4,128)} %param.7) | copy-start | bytes 4468
  0.0 1.1 %copy-start.2 = (s32[16,4]{0,1:T(4,128)S(1)}, s32[16,4]{0,1:T(4,128)}, u32[]{:S(2)}) copy-start(s32[16,4]{0,1:T(4,128)} %param.9) | copy-start | bytes 772
  0.0 1.1 %copy-start.3 = (s32[16]{0:T(128)S(1)}, s32[16]{0:T(128)}, u32[]{:S(2)}) copy-start(s32[16]{0:T(128)} %owner.1) | copy-start | bytes 196

commit v4 on v3

--- a/solution.py
+++ b/solution.py
@@ -247,19 +247,19 @@
         cam.at[:, pl.ds(pl.multiple_of(me * cols, cols), cols)], camrecv.at[me], own_sem
     )
     own.start()
+
+    pl.semaphore_wait(barrier, n - 1)
+    far_first = list(range(1, n))
+    for k in far_first:
+        psf_copy(k).start()
+    for k in far_first:
+        cam_copy(k).start()
     x0 = est[...].T
     xt[...] = x0
     xsend[0, 0:EDGE, :] = x0[cols - EDGE :, :].astype(BF16)
     xsend[0, EDGE:, :] = x0[:EDGE, :].astype(BF16)
     gath[me] = psf[0]
-
-    pl.semaphore_wait(barrier, n - 1)
-    far_first = list(range(1, n))
-    for k in far_first:
-        psf_copy(k).start()
     start(x_copy, 0)
-    for k in far_first:
-        cam_copy(k).start()
 
     lane = lax.broadcasted_iota(jnp.int32, (128, cells), 1)
     line = lax.broadcasted_iota(jnp.int32, (128, cells), 0)

time: 27 us -> 27.8 us (1.030)
  the two profiles are of different devices: /device:TPU:1 before, /device:TPU:13 now
where the time goes in v4:
time: 27.8 us; the launch traced here: 27.7 us
  Pallas kernels  25.9 us (93%)
  local copies, waits for them, and re-layouts  1.76 us (6%)
    pallas_call x1, Pallas kernels, fused_shards(): pl.pallas_call(functools.partial(fused, dims), out_shape=jax.ShapeDtypeSt...  25.9 us
    reshape x1, local copies, waits for them, and re-layouts, fused_shards(): camera_rows.reshape(V * zd * lr, n * cols)  1.08 us
    unnamed x9, local copies, waits for them, and re-layouts  0.67 us

profile of v4, /device:TPU:13, one launch (start us, length us, event | category | flops | bytes accessed | tf_op | source)
XLA Modules:
  0.0 27.7 jit_solution(9678694407022104287)
XLA Ops:
  0.0 0.0 copy-start
  0.0 0.0 copy-start.1
  0.0 0.0 copy-start.2
  0.0 0.0 copy-start.3
  0.0 1.1 %reshape.9.cam = bf16[64,2048]{1,0:T(8,128)(2,1)S(1)} reshape(bf16[4,8,2,2048]{3,2,1,0:T(2,128)(2,1)} %param.5) | data formatting | bytes 524288 | tf_op jit(solution)/shard_map/reshape | solution.py:408
  1.1 0.0 copy-done
  1.1 0.0 copy-done.1
  1.1 0.0 copy-done.2
  1.1 0.0 copy-done.3
  1.1 25.9 %shard_map.55 = f32[256,128]{1,0:T(8,128)S(1)} custom-call(bf16[64,2048]{1,0:T(8,128)(2,1)S(1)} %reshape.9.cam, f32[256,128]{1,0:T(8,128)S(1)} %bitcast.5, f32[1,3,4,31]{3,2,1,0:T(4,128)S(1)} %bitcast.6, s32[16]{0:T(128)S(1)} %copy-done.3, s32[4,16]{1,0:T(4,128)S(1)} %bitcast.7), custom_call_target="tpu_custom_call" | custom-call | tf_op jit(solution)/shard_map/pallas_call | solution.py:379
  27.0 0.7 %copy.7 = f32[8,32,128]{2,1,0:T(8,128)} copy(f32[8,32,128]{2,1,0:T(8,128)S(1)} %bitcast.4) | data formatting | bytes 262144
Async XLA Ops:
  0.0 1.1 %copy-start = (f32[8,32,128]{2,1,0:T(8,128)S(1)}, f32[8,32,128]{2,1,0:T(8,128)}, u32[]{:S(2)}) copy-start(f32[8,32,128]{2,1,0:T(8,128)} %param.6) | copy-start | bytes 393220
  0.0 1.1 %copy-start.1 = (f32[1,4,3,31]{3,1,2,0:T(4,128)S(1)}, f32[1,4,3,31]{3,1,2,0:T(4,128)}, u32[]{:S(2)}) copy-start(f32[1,4,3,31]{3,1,2,0:T(4,128)} %param.7) | copy-start | bytes 4468
  0.0 1.1 %copy-start.2 = (s32[16,4]{0,1:T(4,128)S(1)}, s32[16,4]{0,1:T(4,128)}, u32[]{:S(2)}) copy-start(s32[16,4]{0,1:T(4,128)} %param.9) | copy-start | bytes 772
  0.0 1.1 %copy-start.3 = (s32[16]{0:T(128)S(1)}, s32[16]{0:T(128)}, u32[]{:S(2)}) copy-start(s32[16]{0:T(128)} %owner.1) | copy-start | bytes 196

commit v5 on v3

--- a/solution.py
+++ b/solution.py
@@ -254,11 +254,11 @@
     gath[me] = psf[0]
 
     pl.semaphore_wait(barrier, n - 1)
-    far_first = list(range(1, n))
-    for k in far_first:
+    ring_order = list(range(1, n))
+    start(x_copy, 0)
+    for k in ring_order:
         psf_copy(k).start()
-    start(x_copy, 0)
-    for k in far_first:
+    for k in ring_order:
         cam_copy(k).start()
 
     lane = lax.broadcasted_iota(jnp.int32, (128, cells), 1)

time: 27 us -> 27.1 us (level)
  no operation moved by 1% of the time
where the time goes in v5:
time: 27.1 us; the launch traced here: 26.9 us
  Pallas kernels  25.1 us (93%)
  local copies, waits for them, and re-layouts  1.76 us (6%)
    pallas_call x1, Pallas kernels, fused_shards(): pl.pallas_call(functools.partial(fused, dims), out_shape=jax.ShapeDtypeSt...  25.1 us
    reshape x1, local copies, waits for them, and re-layouts, fused_shards(): camera_rows.reshape(V * zd * lr, n * cols)  1.08 us
    unnamed x9, local copies, waits for them, and re-layouts  0.67 us

profile of v5, /device:TPU:1, one launch (start us, length us, event | category | flops | bytes accessed | tf_op | source)
XLA Modules:
  0.0 26.9 jit_solution(3068458559164380027)
XLA Ops:
  0.0 0.0 copy-start
  0.0 0.0 copy-start.1
  0.0 0.0 copy-start.2
  0.0 0.0 copy-start.3
  0.0 1.1 %reshape.9.cam = bf16[64,2048]{1,0:T(8,128)(2,1)S(1)} reshape(bf16[4,8,2,2048]{3,2,1,0:T(2,128)(2,1)} %param.5) | data formatting | bytes 524288 | tf_op jit(solution)/shard_map/reshape | solution.py:408
  1.1 0.0 copy-done
  1.1 0.0 copy-done.1
  1.1 0.0 copy-done.2
  1.1 0.0 copy-done.3
  1.1 25.1 %shard_map.55 = f32[256,128]{1,0:T(8,128)S(1)} custom-call(bf16[64,2048]{1,0:T(8,128)(2,1)S(1)} %reshape.9.cam, f32[256,128]{1,0:T(8,128)S(1)} %bitcast.5, f32[1,3,4,31]{3,2,1,0:T(4,128)S(1)} %bitcast.6, s32[16]{0:T(128)S(1)} %copy-done.3, s32[4,16]{1,0:T(4,128)S(1)} %bitcast.7), custom_call_target="tpu_custom_call" | custom-call | tf_op jit(solution)/shard_map/pallas_call | solution.py:379
  26.2 0.7 %copy.7 = f32[8,32,128]{2,1,0:T(8,128)} copy(f32[8,32,128]{2,1,0:T(8,128)S(1)} %bitcast.4) | data formatting | bytes 262144
Async XLA Ops:
  0.0 1.1 %copy-start = (f32[8,32,128]{2,1,0:T(8,128)S(1)}, f32[8,32,128]{2,1,0:T(8,128)}, u32[]{:S(2)}) copy-start(f32[8,32,128]{2,1,0:T(8,128)} %param.6) | copy-start | bytes 393220
  0.0 1.1 %copy-start.1 = (f32[1,4,3,31]{3,1,2,0:T(4,128)S(1)}, f32[1,4,3,31]{3,1,2,0:T(4,128)}, u32[]{:S(2)}) copy-start(f32[1,4,3,31]{3,1,2,0:T(4,128)} %param.7) | copy-start | bytes 4468
  0.0 1.1 %copy-start.2 = (s32[16,4]{0,1:T(4,128)S(1)}, s32[16,4]{0,1:T(4,128)}, u32[]{:S(2)}) copy-start(s32[16,4]{0,1:T(4,128)} %param.9) | copy-start | bytes 772
  0.0 1.1 %copy-start.3 = (s32[16]{0:T(128)S(1)}, s32[16]{0:T(128)}, u32[]{:S(2)}) copy-start(s32[16]{0:T(128)} %owner.1) | copy-start | bytes 196
